TPU v7x, 128 devices: a whole 4x4x4 slice. The times are simulated.
128 devices in a mesh: row: 8 (over x, core), col: 16 (over y, z).
Axes of the slice: x: 4, y: 4, z: 4, core: 2. Of those that a mesh axis runs over, the one named last changes fastest.
Arguments:
- leaf_source: float32 [2, 128, 1024, 256], P(None, ('row', 'col')), may hold values from -6 to 6
- leaf_inv: float32 [128, 2, 512, 512], P(('row', 'col')), as said below
- leaf_low: float32 [128, 2, 512, 512], P(('row', 'col')), may hold values from -0.1875 to 0.1875
- child_count: int32 [128], replicated, may hold values from 256 to 512
- child_owner: int32 [128, 512, 1], replicated, may hold values from 0 to 127; in each aligned block of 512 rows (0 to 511, 512 to 1023, ..., all dimensions but the last counted through in order) at most 6 rows name the same one
- child_slot: int32 [128, 512], replicated, may hold values from 0 to 127
- parent_source: float32 [2, 16384, 256], P(None, ('row', 'col')), may hold values from -6 to 6
- parent_inv: float32 [2, 16384, 16384], P(None, 'row', 'col'), as said below
- kernel_coef: float32 [3, 16384], P(None, ('row', 'col')), may hold values from 0.5 to 2
- p_speed: float32 [16384], P(('row', 'col')), may hold values from 1 to 2
- s_speed: float32 [16384], P(('row', 'col')), may hold values from 0.4 to 0.8
- density: float32 [16384], P(('row', 'col')), may hold values from 0.8 to 1.2
Outputs:
- gradient: float32 [3, 16384], P(None, ('row', 'col'))
Inputs may be any that keep to these rules, and one draw needn't show every extreme that they name: `child_owner`: in each aligned block of 512 rows (one child's rows) no owner appears more than 6 times, and some owner appears exactly 6 times. `leaf_inv`: each child's matrix is unit lower triangular: real part 1 and imaginary part 0 on the diagonal, zero above. `parent_inv`: lower triangular in elimination order: stored row p maps to elimination row ((l div 64) * 8 + r) * 64 + l mod 64 with r = p div (2048), l = p mod (2048); stored columns likewise with 16; the diagonal is 1 (real), entries above it zero.
All inputs are finite; a program needn't handle non-finite values.
Results may differ from a plain program's by a relative error of at most 0.00029.
Values sent between devices are 32-bit elements; how exact they have to be, the bound alone decides.
No kernel may reach another device: no remote copies, remote signals or barrier semaphores. Data moves between devices by JAX's collectives and lax.ppermute only.
A program may use at most 128 MiB of HBM per device.

v0:
```python
import jax
import jax.numpy as jnp
from jax import lax
from jax.sharding import PartitionSpec as P

SOURCES = 128


HIGHEST = lax.Precision.HIGHEST


def complex_product(former, latter):

    def single(left_op, right_op):
        return jnp.dot(left_op, right_op, preferred_element_type=jnp.float32, precision=HIGHEST)

    real_part = single(former[0], latter[0]) - single(former[1], latter[1])
    imag_part = single(former[0], latter[1]) + single(former[1], latter[0])
    return jnp.stack([real_part, imag_part])


def material_gradient(eliminated, kernel_coef, p_speed, s_speed, density):
    norming = 1.0 / jnp.sqrt(jnp.float32(SOURCES))
    fwd_real = eliminated[0, :, :SOURCES]
    fwd_imag = eliminated[1, :, :SOURCES]
    adj_real = eliminated[0, :, SOURCES:]
    adj_imag = eliminated[1, :, SOURCES:]
    k_lambda = jnp.sum(fwd_real * adj_real - fwd_imag * adj_imag, axis=1) * norming
    k_mu = jnp.sum(fwd_real * adj_imag + fwd_imag * adj_real, axis=1) * norming
    k_rho = jnp.sum(fwd_real * adj_real + fwd_imag * adj_imag, axis=1) * norming
    grad_lambda = kernel_coef[0] * k_lambda
    grad_mu = kernel_coef[1] * k_mu
    grad_rho = kernel_coef[2] * k_rho
    first_out = 2.0 * density * p_speed * grad_lambda
    second_out = 2.0 * density * s_speed * (grad_mu - 2.0 * grad_lambda)
    third_out = (
        (p_speed * p_speed - 2.0 * s_speed * s_speed) * grad_lambda
        + s_speed * s_speed * grad_mu
        + grad_rho
    )
    return jnp.stack([first_out, second_out, third_out])


def per_device(
    leaf_source,
    leaf_inv,
    leaf_low,
    child_count,
    child_owner,
    child_slot,
    parent_source,
    parent_inv,
    kernel_coef,
    p_speed,
    s_speed,
    density,
):
    row_count = lax.axis_size("row")
    col_count = lax.axis_size("col")
    devices = row_count * col_count
    own_col = lax.axis_index("col")
    myself = lax.axis_index("row") * col_count + own_col
    pivots = leaf_inv.shape[2]
    contrib = leaf_low.shape[2]
    owned_rows = parent_source.shape[1]
    capacity = max(2, 3 * contrib // (2 * devices))
    owners = child_owner[:, :, 0]
    position = jnp.arange(contrib, dtype=jnp.int32)
    live_all = position[None, :] < child_count[:, None]
    my_owner = lax.dynamic_index_in_dim(owners, myself, 0, keepdims=False)
    my_live = lax.dynamic_index_in_dim(live_all, myself, 0, keepdims=False)
    onehot_send = (
        (my_owner[:, None] == jnp.arange(devices, dtype=jnp.int32)[None, :]) & my_live[:, None]
    ).astype(jnp.int32)
    send_rank = jnp.sum((jnp.cumsum(onehot_send, axis=0) - 1) * onehot_send, axis=1)
    slot_index = jnp.where(my_live, my_owner * capacity + send_rank, devices * capacity)
    source_row = (
        jnp.full((devices * capacity + 1,), contrib, jnp.int32)
        .at[slot_index]
        .set(position)[: devices * capacity]
    )
    mine_live = (owners == myself) & live_all
    recv_rank = jnp.cumsum(mine_live.astype(jnp.int32), axis=1) - 1
    column = jnp.where(mine_live, recv_rank, capacity)
    sender_ids = jnp.broadcast_to(jnp.arange(devices, dtype=jnp.int32)[:, None], (devices, contrib))
    local_rows = (
        jnp.full((devices, capacity + 1), -1, jnp.int32)
        .at[sender_ids, column]
        .set(child_slot)[:, :capacity]
    )
    placing = (
        local_rows.reshape(-1)[None, :] == jnp.arange(owned_rows, dtype=jnp.int32)[:, None]
    ).astype(jnp.float32)

    def eliminate(columns_source, parent_part):
        breadth = columns_source.shape[2]
        pivot_part = complex_product(leaf_inv[0], columns_source[:, :pivots])
        update = columns_source[:, pivots:] - complex_product(leaf_low[0], pivot_part)
        padded = jnp.concatenate([update, jnp.zeros((2, 1, breadth), jnp.float32)], axis=1)
        outgoing = padded[:, source_row]
        arrived = lax.all_to_all(
            outgoing.reshape(2, devices, capacity, breadth),
            ("row", "col"),
            split_axis=1,
            concat_axis=1,
            tiled=True,
        )
        arrived = arrived.reshape(2, devices * capacity, breadth)
        assembled = parent_part + jnp.einsum(
            "rk,ckn->crn", placing, arrived, precision=HIGHEST, preferred_element_type=jnp.float32
        )
        partial_value = complex_product(
            parent_inv, lax.all_gather(assembled, "row", axis=1, tiled=True)
        )
        summed = lax.psum(partial_value, "col")
        return lax.dynamic_slice_in_dim(summed, own_col * owned_rows, owned_rows, 1)

    local_source = leaf_source[:, 0]
    forward = eliminate(local_source[:, :, :SOURCES], parent_source[:, :, :SOURCES])
    adjoint = eliminate(local_source[:, :, SOURCES:], parent_source[:, :, SOURCES:])
    eliminated = jnp.concatenate([forward, adjoint], axis=2)
    return material_gradient(eliminated, kernel_coef, p_speed, s_speed, density)


def solution(mesh):
    return jax.shard_map(
        per_device,
        mesh=mesh,
        in_specs=(
            P(None, ("row", "col"), None, None),
            P(("row", "col"), None, None, None),
            P(("row", "col"), None, None, None),
            P(),
            P(),
            P(),
            P(None, ("row", "col"), None),
            P(None, "row", "col"),
            P(None, ("row", "col")),
            P(("row", "col")),
            P(("row", "col")),
            P(("row", "col")),
        ),
        out_specs=P(None, ("row", "col")),
        check_vma=False,
    )
```

profile of v0, /device:TPU:0, one launch (start us, length us, event | category | flops | bytes accessed | tf_op | source)
XLA Modules:
  0.0 532.1 jit_solution(1002658257737356929)
XLA Ops:
  6.5 3.1 copy.59
  9.6 1.9 fusion.72
  11.6 1.9 fusion.70
  13.5 1.9 fusion.76
  15.5 1.9 fusion.74
  21.7 2.7 scatter_custom_fusion
  24.4 2.1 convolution_subtract_fusion.1
  26.5 1.9 convolution_add_fusion.1
  41.8 3.2 gather_fusion
  45.0 11.1 %all-to-all-start = ((f32[2,128,6,128]{3,0,2,1:T(2,128)}), f32[2,128,6,128]{3,0,2,1:T(2,128)S(1)}, u32[]{:S(2)}, u32[]{:S(2)}) async-start(f32[2,128,6,128]{3,0,2,1:T(2,128)} %bitcast.22), calls=%async_computation | async-start | bytes 1572864 | tf_op jit(solution)/shard_map/all_to_all | solution.py:101
  57.8 239.5 %scatter_custom_fusion.1 = s32[896]{0:T(1024)S(1)} fusion(s32[65536]{0:T(1024)S(1)} %bitcast.242, s32[65536]{0:T(1024)S(1)} %bitcast.243, s32[]{:T(128)} %constant.29.clone.1), kind=kCustom, calls=%fused_computation.152 | custom fusion | bytes 3588
  299.6 3.2 gather_fusion.1
  302.8 9.8 %all-to-all-start.1 = ((f32[2,128,6,128]{3,0,2,1:T(2,128)}), f32[2,128,6,128]{3,0,2,1:T(2,128)S(1)}, u32[]{:S(2)}, u32[]{:S(2)}) async-start(f32[2,128,6,128]{3,0,2,1:T(2,128)} %bitcast.46), calls=%async_computation.1 | async-start | bytes 1572864 | tf_op jit(solution)/shard_map/all_to_all | solution.py:101
  312.8 19.0 %all-to-all-done.1 = f32[2,128,6,128]{3,0,2,1:T(2,128)S(1)} async-done(((f32[2,128,6,128]{3,0,2,1:T(2,128)}), f32[2,128,6,128]{3,0,2,1:T(2,128)S(1)}, u32[]{:S(2)}, u32[]{:S(2)}) %all-to-all-start.1) | async-done | bytes 786464 | tf_op jit(solution)/shard_map/all_to_all | solution.py:101
  333.5 11.3 %fusion.6 = f32[128,2048]{1,0:T(8,128)S(1)} fusion(f32[2,2048,1024]{2,1,0:T(8,128)} %param.19, f32[2,1024,128]{1,2,0:T(8,128)} %all-gather.3.cloned.1.call-done), kind=kOutput, calls=%fused_computation.10 | convolution fusion | flops 3221225472 | bytes 9961472 | tf_op jit(solution)/shard_map/dot_general | solution.py:15
  344.9 11.9 %fusion.4 = f32[128,2048]{1,0:T(8,128)S(1)} fusion(f32[2,2048,1024]{2,1,0:T(8,128)} %param.19, f32[2,1024,128]{1,2,0:T(8,128)S(1)} %copy-done.3), kind=kOutput, calls=%fused_computation.8 | convolution fusion | flops 3221225472 | bytes 9961472 | tf_op jit(solution)/shard_map/dot_general | solution.py:15
  356.8 11.5 %fusion.27 = f32[1,2048,128]{1,2,0:T(8,128)S(1)} fusion(f32[128,2048]{1,0:T(8,128)S(1)} %fusion.6, f32[2,2048,1024]{2,1,0:T(8,128)} %param.19, f32[2,1024,128]{1,2,0:T(8,128)S(1)} %copy-done.3), kind=kOutput, calls=%fused_computation.29 | convolution fusion | flops 3221487616 | bytes 11010048 | tf_op jit(solution)/shard_map/dot_general | solution.py:15
  368.3 8.7 %fusion.33 = f32[1,2048,128]{1,2,0:T(8,128)S(1)} fusion(f32[128,2048]{1,0:T(8,128)S(1)} %fusion.4, f32[2,2048,1024]{2,1,0:T(8,128)S(1)} %bitcast.226, f32[2,1024,128]{1,2,0:T(8,128)S(1)} %copy-done.3), kind=kOutput, calls=%fused_computation.31 | convolution fusion | flops 3221487616 | bytes 11010048 | tf_op jit(solution)/shard_map/dot_general | solution.py:15
  378.6 11.3 %fusion.2 = f32[128,2048]{1,0:T(8,128)S(1)} fusion(f32[2,2048,1024]{2,1,0:T(8,128)} %param.19, f32[2,1024,128]{1,2,0:T(8,128)} %all-gather.5.cloned.1.call-done), kind=kOutput, calls=%fused_computation.6 | convolution fusion | flops 3221225472 | bytes 9961472 | tf_op jit(solution)/shard_map/dot_general | solution.py:15
  389.9 12.2 %fusion = f32[128,2048]{1,0:T(8,128)S(1)} fusion(f32[2,2048,1024]{2,1,0:T(8,128)} %param.19, f32[2,1024,128]{1,2,0:T(8,128)S(1)} %copy-done.4), kind=kOutput, calls=%fused_computation.4 | convolution fusion | flops 3221225472 | bytes 9961472 | tf_op jit(solution)/shard_map/dot_general | solution.py:15
  402.2 11.5 %fusion.39 = f32[1,2048,128]{1,2,0:T(8,128)S(1)} fusion(f32[128,2048]{1,0:T(8,128)S(1)} %fusion.2, f32[2,2048,1024]{2,1,0:T(8,128)} %param.19, f32[2,1024,128]{1,2,0:T(8,128)S(1)} %copy-done.4), kind=kOutput, calls=%fused_computation.33 | convolution fusion | flops 3221487616 | bytes 11010048 | tf_op jit(solution)/shard_map/dot_general | solution.py:15
  413.7 8.8 %fusion.45 = f32[1,2048,128]{1,2,0:T(8,128)S(1)} fusion(f32[128,2048]{1,0:T(8,128)S(1)} %fusion, f32[2,2048,1024]{2,1,0:T(8,128)S(1)} %bitcast.228, f32[2,1024,128]{1,2,0:T(8,128)S(1)} %copy-done.4), kind=kOutput, calls=%fused_computation.35 | convolution fusion | flops 3221487616 | bytes 11010048 | tf_op jit(solution)/shard_map/dot_general | solution.py:15
  422.5 1.5 pad_maximum_fusion.1
  424.0 99.4 %all-reduce.5.cloned.1.call-done = (f32[2,2048,128]{1,2,0:T(8,128)}, f32[2,2048,128]{1,2,0:T(8,128)}) async-done(((f32[2,2048,128]{1,2,0:T(8,128)}, f32[2,2048,128]{1,2,0:T(8,128)}), (f32[2,2048,128]{1,2,0:T(8,128)}, f32[2,2048,128]{1,2,0:T(8,128)})) %all-reduce.5.cloned.1.call-update) | async-done | bytes 4194320 | tf_op jit(solution)/shard_map/psum | solution.py:115
  (116 shorter events, 26.2 us)
Async XLA Ops:
  6.5 3.1 copy-start
  11.6 5.8 %copy-start.8 = (s32[128]{0:T(128)S(1)}, s32[128]{0:T(128)}, u32[]{:S(2)}) copy-start(s32[128]{0:T(128)} %param.15) | copy-start | bytes 1540
  24.4 4.1 copy-start.1
  41.6 14.7 %copy-start.5 = (s32[128,512,1]{1,2,0:T(1,128)S(1)}, s32[128,512,1]{1,2,0:T(1,128)}, u32[]{:S(2)}) copy-start(s32[128,512,1]{1,2,0:T(1,128)} %param.16) | copy-start | bytes 786436
  45.0 252.7 %all-to-all-start = ((f32[2,128,6,128]{3,0,2,1:T(2,128)}), f32[2,128,6,128]{3,0,2,1:T(2,128)S(1)}, u32[]{:S(2)}, u32[]{:S(2)}) async-start(f32[2,128,6,128]{3,0,2,1:T(2,128)} %bitcast.22), calls=%async_computation | async-start | bytes 1572864 | tf_op jit(solution)/shard_map/all_to_all | solution.py:101
  56.2 277.3 %all-gather.3.cloned.1.call-start = ((), (), s32[]{:S(2)}) async-start(), calls=%async_computation.2 | async-start | bytes 1179648 | tf_op jit(solution)/shard_map/all_gather | solution.py:113
  56.9 240.7 %copy-start.7 = (f32[2,128,256]{2,1,0:T(8,128)S(1)}, f32[2,128,256]{2,1,0:T(8,128)}, u32[]{:S(2)}) copy-start(f32[2,128,256]{2,1,0:T(8,128)} %param.18) | copy-start | bytes 786436
  302.8 28.9 %all-to-all-start.1 = ((f32[2,128,6,128]{3,0,2,1:T(2,128)}), f32[2,128,6,128]{3,0,2,1:T(2,128)S(1)}, u32[]{:S(2)}, u32[]{:S(2)}) async-start(f32[2,128,6,128]{3,0,2,1:T(2,128)} %bitcast.46), calls=%async_computation.1 | async-start | bytes 1572864 | tf_op jit(solution)/shard_map/all_to_all | solution.py:101
  312.6 66.0 %all-gather.5.cloned.1.call-start = ((), (), s32[]{:S(2)}) async-start(), calls=%async_computation.3 | async-start | bytes 1179648 | tf_op jit(solution)/shard_map/all_gather | solution.py:113
  333.2 190.2 %all-reduce.5.cloned.1.call-start = ((), (), s32[]{:S(2)}) async-start(), calls=%async_computation.4 | async-start | bytes 8388608 | tf_op jit(solution)/shard_map/psum | solution.py:115
  333.5 11.4 %copy-start.3 = (f32[2,1024,128]{1,2,0:T(8,128)S(1)}, f32[2,1024,128]{1,2,0:T(8,128)}, u32[]{:S(2)}) copy-start(f32[2,1024,128]{1,2,0:T(8,128)} %all-gather.3.cloned.1.call-done) | copy-start | bytes 3145732
  333.5 34.8 %slice-start = ((s8[16777216]{0:T(1024)(128)(4,1)}), s8[4194304]{0:T(1024)(128)(4,1)S(1)}, s32[]{:S(2)}) async-start(s8[16777216]{0:T(1024)(128)(4,1)} %bitcast.225), calls=%async_computation.5 | async-start | bytes 8388608
  333.5 34.8 %slice-start.1 = ((s8[16777216]{0:T(1024)(128)(4,1)}), s8[4194304]{0:T(1024)(128)(4,1)S(1)}, s32[]{:S(2)}) async-start(s8[16777216]{0:T(1024)(128)(4,1)} %bitcast.225), calls=%async_computation.6 | async-start | bytes 8388608
  344.9 23.5 %slice-start.2 = ((s8[16777216]{0:T(1024)(128)(4,1)}), s8[4194304]{0:T(1024)(128)(4,1)S(1)}, s32[]{:S(2)}) async-start(s8[16777216]{0:T(1024)(128)(4,1)} %bitcast.225), calls=%async_computation.7 | async-start | bytes 8388608
  356.8 11.5 %slice-start.3 = ((s8[16777216]{0:T(1024)(128)(4,1)}), s8[4194304]{0:T(1024)(128)(4,1)S(1)}, s32[]{:S(2)}) async-start(s8[16777216]{0:T(1024)(128)(4,1)} %bitcast.225), calls=%async_computation.8 | async-start | bytes 8388608
  378.6 11.3 %copy-start.4 = (f32[2,1024,128]{1,2,0:T(8,128)S(1)}, f32[2,1024,128]{1,2,0:T(8,128)}, u32[]{:S(2)}) copy-start(f32[2,1024,128]{1,2,0:T(8,128)} %all-gather.5.cloned.1.call-done) | copy-start | bytes 3145732
  378.6 35.1 %slice-start.4 = ((s8[16777216]{0:T(1024)(128)(4,1)}), s8[4194304]{0:T(1024)(128)(4,1)S(1)}, s32[]{:S(2)}) async-start(s8[16777216]{0:T(1024)(128)(4,1)} %bitcast.227), calls=%async_computation.9 | async-start | bytes 8388608
  378.6 35.1 %slice-start.5 = ((s8[16777216]{0:T(1024)(128)(4,1)}), s8[4194304]{0:T(1024)(128)(4,1)S(1)}, s32[]{:S(2)}) async-start(s8[16777216]{0:T(1024)(128)(4,1)} %bitcast.227), calls=%async_computation.10 | async-start | bytes 8388608
  389.9 23.8 %slice-start.6 = ((s8[16777216]{0:T(1024)(128)(4,1)}), s8[4194304]{0:T(1024)(128)(4,1)S(1)}, s32[]{:S(2)}) async-start(s8[16777216]{0:T(1024)(128)(4,1)} %bitcast.227), calls=%async_computation.11 | async-start | bytes 8388608
  402.1 11.6 %slice-start.7 = ((s8[16777216]{0:T(1024)(128)(4,1)}), s8[4194304]{0:T(1024)(128)(4,1)S(1)}, s32[]{:S(2)}) async-start(s8[16777216]{0:T(1024)(128)(4,1)} %bitcast.227), calls=%async_computation.12 | async-start | bytes 8388608
  424.0 100.5 %copy-start.9 = (f32[3,128]{1,0:T(4,128)S(1)}, f32[3,128]{1,0:T(4,128)}, u32[]{:S(2)}) copy-start(f32[3,128]{1,0:T(4,128)} %param.20) | copy-start | bytes 4612
  424.0 100.5 %copy-start.10 = (f32[128]{0:T(128)S(1)}, f32[128]{0:T(128)}, u32[]{:S(2)}) copy-start(f32[128]{0:T(128)} %param.22) | copy-start | bytes 1540
  424.0 100.5 %copy-start.11 = (f32[128]{0:T(128)S(1)}, f32[128]{0:T(128)}, u32[]{:S(2)}) copy-start(f32[128]{0:T(128)} %param.23) | copy-start | bytes 1540
  424.0 100.5 %copy-start.12 = (f32[128]{0:T(128)S(1)}, f32[128]{0:T(128)}, u32[]{:S(2)}) copy-start(f32[128]{0:T(128)} %param.21) | copy-start | bytes 1540
  (4 other events, 5.2 us)
Sparse Core Ops, SparseCore 0:
  299.3 28.2 all-gather.2
  333.4 19.6 all-gather.4
  424.1 99.2 all-reduce.4
where the time goes:
time: 538 us; the launch traced here: 532 us
  local copies, waits for them, and re-layouts  255 us (47%)
  waiting for transfers between devices  119 us (22%)
  matrix products  114 us (21%)
  starting transfers between devices  21.2 us (4%)
  between operations  14.4 us (3%)
  other arithmetic  8.63 us (2%)
    unnamed x56, local copies, waits for them, and re-layouts  244 us
    dot_general x24, matrix products, single(): jnp.dot(left_op, right_op, preferred_element_type=jnp.float32, precision=...  111 us
    psum x1, waiting for transfers between devices, eliminate(): summed = lax.psum(partial_value, 'col')  99.4 us
    all_to_all x2, starting transfers between devices, eliminate(): lax.all_to_all(outgoing.reshape(2, devices, capacity, breadth), ('row', '...  20.9 us
    all_to_all x2, waiting for transfers between devices, eliminate(): lax.all_to_all(outgoing.reshape(2, devices, capacity, breadth), ('row', '...  19 us
  transfers between devices with their start and end apart: 5, of which 2 were waited for; matrix products, arithmetic and copies ran while one was open for 55% of the time, Pallas kernels for 0%

commit v1 on v0

v1 whole, which is shorter than its diff:
```python
import functools

import jax
import jax.numpy as jnp
from jax import lax
from jax.experimental import pallas as pl
from jax.experimental.pallas import tpu as pltpu
from jax.sharding import PartitionSpec as P

SOURCES = 128
CAPACITY = 6
LANES = 128
RING = 4
F32 = jnp.float32
BF16 = jnp.bfloat16


def halves(value):
    high = value.astype(BF16)
    return high, (value - high.astype(F32)).astype(BF16)


def dot(left, right, dims=((1,), (0,))):
    return lax.dot_general(left, right, (dims, ((), ())), preferred_element_type=F32)


def dot3(left, right_high, right_low):
    left_high, left_low = halves(left)
    return dot(left_high, right_high) + (dot(left_high, right_low) + dot(left_low, right_high))


def complex_rows(real_left, imag_left, right):
    breadth = right.shape[1] // 2
    high, low = halves(right)
    by_real = dot3(real_left, high, low)
    by_imag = dot3(imag_left, high, low)
    real_part = by_real[:, :breadth] - by_imag[:, breadth:]
    imag_part = by_real[:, breadth:] + by_imag[:, :breadth]
    return real_part, imag_part


def running_count(mask):
    length = mask.shape[1]
    former = lax.broadcasted_iota(jnp.int32, (length, length), 0)
    latter = lax.broadcasted_iota(jnp.int32, (length, length), 1)
    upto = jnp.where(former <= latter, 1.0, 0.0).astype(BF16)
    return dot(mask.astype(BF16), upto)


def leaf_kernel(place, owner_ref, source_ref, inv_ref, low_ref, out_ref):
    pivots = inv_ref.shape[1]
    devices = owner_ref.shape[0]
    contrib = owner_ref.shape[1]
    pivot_source = jnp.concatenate([source_ref[0, :pivots], source_ref[1, :pivots]], axis=1)
    pivot_part = jnp.concatenate(complex_rows(inv_ref[0], inv_ref[1], pivot_source), axis=1)
    real_low, imag_low = complex_rows(low_ref[0], low_ref[1], pivot_part)
    update = jnp.concatenate(
        [source_ref[0, pivots:] - real_low, source_ref[1, pivots:] - imag_low], axis=1
    )
    high, low = halves(update)
    my_owner = owner_ref[pl.ds(place[0], 1), :]
    names = lax.broadcasted_iota(jnp.int32, (devices, contrib), 0)
    chosen = jnp.where(names == my_owner, 1.0, 0.0)
    rank = running_count(chosen) * chosen
    groups = update.shape[1] // LANES
    for k in range(CAPACITY):
        pick = jnp.where(rank == k + 1.0, 1.0, 0.0).astype(BF16)
        rows = dot(pick, high) + dot(pick, low)
        for g in range(groups):
            out_ref[pl.ds(k * groups + g, devices, stride=CAPACITY * groups), :] = rows[
                :, g * LANES : (g + 1) * LANES
            ]


def placing_kernel(place, owner_ref, slot_ref, out_ref):
    devices = owner_ref.shape[0]
    owned = out_ref.shape[2]
    mine = jnp.where(owner_ref[...] == place[0], 1.0, 0.0)
    rank = running_count(mine) * mine
    slots = slot_ref[...].astype(F32) + 1.0
    rows = lax.broadcasted_iota(jnp.int32, (devices, owned), 1).astype(F32) + 1.0
    for k in range(CAPACITY):
        slot = jnp.sum(jnp.where(rank == k + 1.0, slots, 0.0), axis=1, keepdims=True)
        out_ref[k] = jnp.where(slot == rows, 1.0, 0.0).astype(BF16)


def extend_kernel(placing_ref, arrived_ref, parent_ref, out_ref):
    devices = placing_ref.shape[1]
    groups = out_ref.shape[1] // LANES
    breadth = parent_ref.shape[2]
    for g in range(groups):
        at = g * LANES
        total = parent_ref[at // breadth, :, at % breadth : at % breadth + LANES]
        for k in range(CAPACITY):
            rows = arrived_ref[pl.ds(k * groups + g, devices, stride=CAPACITY * groups), :]
            high, low = halves(rows)
            total += dot(placing_ref[k], high, ((0,), (0,)))
            total += dot(placing_ref[k], low, ((0,), (0,)))
        out_ref[:, at : at + LANES] = total


def parent_kernel(place, inv_ref, own_ref, other_ref, left_ref, right_ref, far_ref, swapped_ref, *rest):
    along_y, along_z, (high_ref, low_ref) = rest[:RING], rest[RING : 2 * RING], rest[2 * RING :]
    step = pl.program_id(0)
    owned, width = own_ref.shape
    breadth = width // 2
    depth = 2 * owned
    block = inv_ref.shape[1]
    own_x, own_core, own_y, own_z = place[1], place[2], place[3], place[4]

    @pl.when(step == 0)
    def _():
        def fill(value, from_x, core):
            at = pl.multiple_of((lax.rem(from_x + RING, RING) * 2 + core) * owned, owned)
            high, low = halves(value)
            high_ref[pl.ds(at, owned), :] = high
            low_ref[pl.ds(at, owned), :] = low

        fill(own_ref[...], own_x, own_core)
        fill(other_ref[...], own_x, 1 - own_core)
        for at, (hop, ref) in enumerate(((1, left_ref), (3, right_ref), (2, far_ref))):
            fill(ref[...], own_x - hop, own_core)
            fill(swapped_ref[at], own_x - hop, 1 - own_core)

    def finish(total_real, total_imag):
        for j in range(block // owned):
            column = step * (block // owned) + j
            hop_y = lax.rem(column // RING - own_y + RING, RING)
            hop_z = lax.rem(lax.rem(column, RING) - own_z + RING, RING)
            rows = slice(j * owned, (j + 1) * owned)
            real_part, imag_part = total_real[rows], total_imag[rows]
            forward = jnp.concatenate([real_part[:, :SOURCES], imag_part[:, :SOURCES]], axis=1)
            adjoint = jnp.concatenate([real_part[:, SOURCES:], imag_part[:, SOURCES:]], axis=1)
            for hop in range(RING):

                @pl.when(hop_y == hop)
                def _(hop=hop):
                    along_y[hop][hop_z] = forward

                @pl.when(hop_z == hop)
                def _(hop=hop):
                    along_z[hop][hop_y] = adjoint

    pieces = inv_ref.shape[2] // depth
    for reach in range(pieces):

        @pl.when(step * block // (2 * depth) == reach)
        def _(reach=reach):
            deep = (reach + 1) * depth
            high, low = high_ref[:deep], low_ref[:deep]
            by_real = dot3(inv_ref[0, :, :deep], high, low)
            by_imag = dot3(inv_ref[1, :, :deep], high, low)
            finish(
                by_real[:, :breadth] - by_imag[:, breadth:],
                by_real[:, breadth:] + by_imag[:, :breadth],
            )


def material_gradient(forward, adjoint, kernel_coef, p_speed, s_speed, density):
    norming = 1.0 / jnp.sqrt(jnp.float32(SOURCES))
    fwd_real, fwd_imag = forward[:, :SOURCES], forward[:, SOURCES:]
    adj_real, adj_imag = adjoint[:, :SOURCES], adjoint[:, SOURCES:]
    k_lambda = jnp.sum(fwd_real * adj_real - fwd_imag * adj_imag, axis=1) * norming
    k_mu = jnp.sum(fwd_real * adj_imag + fwd_imag * adj_real, axis=1) * norming
    k_rho = jnp.sum(fwd_real * adj_real + fwd_imag * adj_imag, axis=1) * norming
    grad_lambda = kernel_coef[0] * k_lambda
    grad_mu = kernel_coef[1] * k_mu
    grad_rho = kernel_coef[2] * k_rho
    first_out = 2.0 * density * p_speed * grad_lambda
    second_out = 2.0 * density * s_speed * (grad_mu - 2.0 * grad_lambda)
    third_out = (
        (p_speed * p_speed - 2.0 * s_speed * s_speed) * grad_lambda
        + s_speed * s_speed * grad_mu
        + grad_rho
    )
    return jnp.stack([first_out, second_out, third_out])


def along(axis, hop):
    if axis == "core":
        return [(i, i ^ 1) for i in range(2 * RING)]
    if axis == "x":
        return [(i, (i + 2 * hop) % (2 * RING)) for i in range(2 * RING)]
    if axis == "y":
        return [(i, (i + RING * hop) % (RING * RING)) for i in range(RING * RING)]
    return [(i, i // RING * RING + (i + hop) % RING) for i in range(RING * RING)]


def move(value, axis, hop=1):
    return lax.ppermute(value, "row" if axis in ("x", "core") else "col", along(axis, hop))


def params(mebibytes, **more):
    return pltpu.CompilerParams(vmem_limit_bytes=mebibytes << 20, **more)


SMEM = pl.BlockSpec(memory_space=pltpu.SMEM)
VMEM = pl.BlockSpec(memory_space=pltpu.VMEM)


def per_device(
    leaf_source,
    leaf_inv,
    leaf_low,
    child_count,
    child_owner,
    child_slot,
    parent_source,
    parent_inv,
    kernel_coef,
    p_speed,
    s_speed,
    density,
):
    row, col = lax.axis_index("row"), lax.axis_index("col")
    devices = lax.axis_size("row") * lax.axis_size("col")
    owned = parent_source.shape[1]
    width = 2 * parent_source.shape[2]
    place = jnp.stack([row * lax.axis_size("col") + col, row // 2, row % 2, col // RING, col % RING])
    position = jnp.arange(child_slot.shape[1], dtype=jnp.int32)
    owner = jnp.where(position[None, :] < child_count[:, None], child_owner[:, :, 0], -1)

    outgoing = pl.pallas_call(
        leaf_kernel,
        out_shape=jax.ShapeDtypeStruct((devices * CAPACITY * width // LANES, LANES), F32),
        in_specs=[SMEM] + [VMEM] * 4,
        out_specs=VMEM,
        compiler_params=params(40),
        name="leaf",
    )(place, owner, leaf_source[:, 0], leaf_inv[0], leaf_low[0])
    placing = pl.pallas_call(
        placing_kernel,
        out_shape=jax.ShapeDtypeStruct((CAPACITY, devices, owned), BF16),
        in_specs=[SMEM] + [VMEM] * 2,
        out_specs=VMEM,
        compiler_params=params(16),
        cost_estimate=pl.CostEstimate(flops=2 * devices * 512 * 512, bytes_accessed=1 << 20, transcendentals=0),
        name="placing",
    )(place, owner, child_slot)
    arrived = lax.all_to_all(
        outgoing.reshape(devices, -1, LANES), ("row", "col"), split_axis=0, concat_axis=0, tiled=True
    )
    assembled = pl.pallas_call(
        extend_kernel,
        out_shape=jax.ShapeDtypeStruct((owned, width), F32),
        in_specs=[VMEM] * 3,
        out_specs=VMEM,
        compiler_params=params(16),
        name="extend",
    )(placing, arrived.reshape(outgoing.shape), parent_source)

    other = move(assembled, "core")
    hops = [move(assembled, "x", hop) for hop in (1, 3, 2)]
    swapped = move(jnp.stack(hops), "core")

    block = 2 * owned
    steps = parent_inv.shape[1] // block
    piece = jax.ShapeDtypeStruct((RING, owned, width // 2), F32)
    whole = pl.BlockSpec((RING, owned, width // 2), lambda i: (0, 0, 0))
    part = pl.BlockSpec((owned, width), lambda i: (0, 0))
    sums = pl.pallas_call(
        parent_kernel,
        out_shape=[piece] * (2 * RING),
        grid=(steps,),
        in_specs=[
            SMEM,
            pl.BlockSpec((2, block, parent_inv.shape[2]), lambda i: (0, i, 0)),
            part, part, part, part, part,
            pl.BlockSpec((3, owned, width), lambda i: (0, 0, 0)),
        ],
        out_specs=[whole] * (2 * RING),
        scratch_shapes=[pltpu.VMEM((parent_inv.shape[2], width), BF16)] * 2,
        compiler_params=params(48),
        name="parent",
    )(place, parent_inv, assembled, other, *hops, swapped)
    along_y, along_z = sums[:RING], sums[RING:]

    hop_order = (1, 3, 2)
    from_y = [move(along_y[hop], "y", hop) for hop in hop_order]
    from_z = [move(along_z[hop], "z", hop) for hop in hop_order]
    plane_y = along_y[0] + from_y[0] + from_y[1] + from_y[2]
    plane_z = along_z[0] + from_z[0] + from_z[1] + from_z[2]
    then_z = [move(plane_y[hop], "z", hop) for hop in hop_order]
    then_y = [move(plane_z[hop], "y", hop) for hop in hop_order]
    forward = plane_y[0] + then_z[0] + then_z[1] + then_z[2]
    adjoint = plane_z[0] + then_y[0] + then_y[1] + then_y[2]
    return material_gradient(forward, adjoint, kernel_coef, p_speed, s_speed, density)


def solution(mesh):
    return jax.shard_map(
        per_device,
        mesh=mesh,
        in_specs=(
            P(None, ("row", "col"), None, None),
            P(("row", "col"), None, None, None),
            P(("row", "col"), None, None, None),
            P(),
            P(),
            P(),
            P(None, ("row", "col"), None),
            P(None, "row", "col"),
            P(None, ("row", "col")),
            P(("row", "col")),
            P(("row", "col")),
            P(("row", "col")),
        ),
        out_specs=P(None, ("row", "col")),
        check_vma=False,
    )
```

time: 538 us -> 134 us (0.25)
  local copies, waits for them, and re-layouts: 255 us -> 5.81 us
  matrix products: 114 us -> 0 us
  waiting for transfers between devices: 119 us -> 71.5 us
  Pallas kernels: 0 us -> 22.3 us
  between operations: 14.4 us -> 0.17 us
  starting transfers between devices: 21.2 us -> 31.5 us
  other arithmetic: 8.63 us -> 2.18 us
    unnamed x56 -> x20, local copies, waits for them, and re-layouts: 244 us -> 5.67 us
    dot_general x26 -> x0, matrix products: 114 us -> none  [the longest x24 111 us: single(): jnp.dot(left_op, right_op, preferred_element_type=jnp.float32, precision=...]
    psum x1 -> x0, waiting for transfers between devices: 99.4 us -> none  [eliminate(): summed = lax.psum(partial_value, 'col')]
    ppermute x0 -> x17, waiting for transfers between devices: none -> 48 us  [move(): lax.ppermute(value, 'row' if axis in ('x', 'core') else 'col', along(axis...]
    pallas_call x0 -> x4, Pallas kernels: none -> 22.3 us  [the longest x1 14.2 us: per_device(): pl.pallas_call(parent_kernel, out_shape=[piece] * (2 * RING), grid=(steps...]
    ppermute x0 -> x17, starting transfers between devices: none -> 20.3 us  [move(): lax.ppermute(value, 'row' if axis in ('x', 'core') else 'col', along(axis...]
    all_to_all x2 -> x1, starting transfers between devices: 20.9 us -> 11.1 us  [per_device(): lax.all_to_all(outgoing.reshape(devices, -1, LANES), ('row', 'col'), spli...]
    gather x2 -> x0, local copies, waits for them, and re-layouts: 6.47 us -> none  [eliminate(): outgoing = padded[:, source_row]]
  transfers between devices with their start and end apart: 5 -> 18, of which waited for: 2 -> 10; matrix products, arithmetic and copies ran while one was open for 55% -> 0% of each run, Pallas kernels for 0% -> 1%
where the time goes in v1:
time: 134 us; the launch traced here: 133 us
  waiting for transfers between devices  71.5 us (53%)
  starting transfers between devices  31.5 us (24%)
  Pallas kernels  22.3 us (17%)
  local copies, waits for them, and re-layouts  5.81 us (4%)
  other arithmetic  2.18 us (2%)
    ppermute x17, waiting for transfers between devices, move(): lax.ppermute(value, 'row' if axis in ('x', 'core') else 'col', along(axis...  48 us
    all_to_all x1, waiting for transfers between devices, per_device(): lax.all_to_all(outgoing.reshape(devices, -1, LANES), ('row', 'col'), spli...  23.5 us
    ppermute x17, starting transfers between devices, move(): lax.ppermute(value, 'row' if axis in ('x', 'core') else 'col', along(axis...  20.3 us
    pallas_call x1, Pallas kernels, per_device(): pl.pallas_call(parent_kernel, out_shape=[piece] * (2 * RING), grid=(steps...  14.2 us
    all_to_all x1, starting transfers between devices, per_device(): lax.all_to_all(outgoing.reshape(devices, -1, LANES), ('row', 'col'), spli...  11.1 us
    pallas_call x1, Pallas kernels, per_device(): pl.pallas_call(leaf_kernel, out_shape=jax.ShapeDtypeStruct((devices * CAP...  6.4 us
    unnamed x20, local copies, waits for them, and re-layouts  5.67 us
  transfers between devices with their start and end apart: 18, of which 10 were waited for; matrix products, arithmetic and copies ran while one was open for 0% of the time, Pallas kernels for 1%

profile of v1, /device:TPU:0, one launch (start us, length us, event | category | flops | bytes accessed | tf_op | source)
XLA Modules:
  0.0 133.4 jit_solution(15920751707119950553)
XLA Ops:
  0.0 1.0 bitcast_select_fusion.owner_ref
  1.1 1.6 %copy-done = f32[2,1,1024,256]{3,2,1,0:T(8,128)S(1)} copy-done((f32[2,1,1024,256]{3,2,1,0:T(8,128)S(1)}, f32[2,1,1024,256]{3,2,1,0:T(8,128)}, u32[]{:S(2)}) %copy-start) | copy-done | bytes 2097176
  2.7 1.6 %copy-done.1 = f32[1,2,512,512]{3,2,1,0:T(8,128)S(1)} copy-done((f32[1,2,512,512]{3,2,1,0:T(8,128)S(1)}, f32[1,2,512,512]{3,2,1,0:T(8,128)}, u32[]{:S(2)}) %copy-start.1) | copy-done | bytes 2097176
  4.3 1.6 %copy-done.2 = f32[1,2,512,512]{3,2,1,0:T(8,128)S(1)} copy-done((f32[1,2,512,512]{3,2,1,0:T(8,128)S(1)}, f32[1,2,512,512]{3,2,1,0:T(8,128)}, u32[]{:S(2)}) %copy-start.2) | copy-done | bytes 2097176
  5.9 6.4 %leaf.1 = f32[3072,128]{1,0:T(8,128)} custom-call(s32[5]{0:T(128)S(1)} %stack.47.place, s32[128,512]{1,0:T(8,128)S(1)} %bitcast_select_fusion.owner_ref, f32[2,1024,256]{2,1,0:T(8,128)S(1)} %bitcast.70, f32[2,512,512]{2,1,0:T(8,128)S(1)} %bitcast.71, f32[2,512,512]{2,1,0:T(8,128)S(1)} %bitcast.72), custom_call_target="tpu_custom_call" | custom-call | tf_op jit(solution)/shard_map/leaf/pallas_call | solution.py:223
  12.3 11.1 %all-to-all-start = ((f32[128,24,128]{2,1,0:T(8,128)}), f32[128,24,128]{2,1,0:T(8,128)S(1)}, u32[]{:S(2)}, u32[]{:S(2)}) async-start(f32[128,24,128]{2,1,0:T(8,128)} %bitcast.9), calls=%async_computation | async-start | bytes 3145728 | tf_op jit(solution)/shard_map/all_to_all | solution.py:240
  23.5 1.0 placing.1.placing_ref
  24.5 23.5 %all-to-all-done = f32[128,24,128]{2,1,0:T(8,128)S(1)} async-done(((f32[128,24,128]{2,1,0:T(8,128)}), f32[128,24,128]{2,1,0:T(8,128)S(1)}, u32[]{:S(2)}, u32[]{:S(2)}) %all-to-all-start) | async-done | bytes 1572896 | tf_op jit(solution)/shard_map/all_to_all | solution.py:240
  49.5 2.7 %collective-permute-start.2 = (f32[128,512]{1,0:T(8,128)S(1)}, f32[128,512]{1,0:T(8,128)S(1)}, u32[]{:S(2)}, u32[]{:S(2)}) collective-permute-start(f32[128,512]{1,0:T(8,128)S(1)} %extend.1.own_ref), channel_id=1, source_target_pairs={{0,96},{16,112},{32,0},{48,16},{64,32},{80,48},{96,64},{112,80},{1... | collective-permute-start | bytes 786440 | tf_op jit(solution)/shard_map/ppermute | solution.py:190
  52.1 7.3 %collective-permute-done.3.far_ref = f32[128,512]{1,0:T(8,128)S(1)} collective-permute-done((f32[128,512]{1,0:T(8,128)S(1)}, f32[128,512]{1,0:T(8,128)S(1)}, u32[]{:S(2)}, u32[]{:S(2)}) %collective-permute-start.3) | collective-permute-done | bytes 262176 | tf_op jit(solution)/shard_map/ppermute | solution.py:190
  59.4 2.4 %collective-permute-done.2.right_ref = f32[128,512]{1,0:T(8,128)S(1)} collective-permute-done((f32[128,512]{1,0:T(8,128)S(1)}, f32[128,512]{1,0:T(8,128)S(1)}, u32[]{:S(2)}, u32[]{:S(2)}) %collective-permute-start.2) | collective-permute-done | bytes 262176 | tf_op jit(solution)/shard_map/ppermute | solution.py:190
  61.8 1.1 collective-permute-done.1.left_ref
  63.5 2.1 %collective-permute-done.other_ref = f32[128,512]{1,0:T(8,128)S(1)} collective-permute-done((f32[128,512]{1,0:T(8,128)S(1)}, f32[128,512]{1,0:T(8,128)S(1)}, u32[]{:S(2)}, u32[]{:S(2)}) %collective-permute-start) | collective-permute-done | bytes 262176 | tf_op jit(solution)/shard_map/ppermute | solution.py:190
  66.6 14.2 %parent.1 = (f32[4,128,256]{2,1,0:T(8,128)S(1)}, f32[4,128,256]{2,1,0:T(8,128)S(1)}, f32[4,128,256]{2,1,0:T(8,128)S(1)}, f32[4,128,256]{2,1,0:T(8,128)S(1)}, f32...) custom-call(s32[5]{0:T(128)S(1)} %stack.47.place, ...), custom_call_target="tpu_custom_call" | custom-call | tf_op jit(solution)/shard_map/parent/pallas_call | solution.py:261
  80.8 1.0 collective-permute-start.5
  81.8 2.3 %collective-permute-start.6 = (f32[4,128,256]{2,1,0:T(8,128)S(1)}, f32[4,128,256]{2,1,0:T(8,128)S(1)}, u32[]{:S(2)}, u32[]{:S(2)}) collective-permute-start(f32[4,128,256]{2,1,0:T(8,128)S(1)} %get-tuple-element.15), channel_id=1, source_target_pairs={{0,12},{1,13},{2,14},{3,15},{4,0},{5,1},{6,2},{7,3},{8,4},{9,5},{1... | collective-permute-start | bytes 1572872 | tf_op jit(solution)/shard_map/ppermute | solution.py:190
  84.1 1.0 collective-permute-start.7
  86.0 2.4 %collective-permute-start.12 = (f32[4,128,256]{2,1,0:T(8,128)S(1)}, f32[4,128,256]{2,1,0:T(8,128)S(1)}, u32[]{:S(2)}, u32[]{:S(2)}) collective-permute-start(f32[4,128,256]{2,1,0:T(8,128)S(1)} %get-tuple-element.19), channel_id=1, source_target_pairs={{0,3},{1,0},{2,1},{3,2},{4,7},{5,4},{6,5},{7,6},{8,11},{9,8},{10,9... | collective-permute-start | bytes 1572872 | tf_op jit(solution)/shard_map/ppermute | solution.py:190
  88.4 18.9 %collective-permute-done.5 = f32[4,128,256]{2,1,0:T(8,128)S(1)} collective-permute-done((f32[4,128,256]{2,1,0:T(8,128)S(1)}, f32[4,128,256]{2,1,0:T(8,128)S(1)}, u32[]{:S(2)}, u32[]{:S(2)}) %collective-permute-start.5) | collective-permute-done | bytes 524320 | tf_op jit(solution)/shard_map/ppermute | solution.py:190
  107.3 2.2 %collective-permute-start.13 = (f32[4,128,256]{2,1,0:T(8,128)S(1)}, f32[4,128,256]{2,1,0:T(8,128)S(1)}, u32[]{:S(2)}, u32[]{:S(2)}) collective-permute-start(f32[4,128,256]{2,1,0:T(8,128)S(1)} %get-tuple-element.20), channel_id=1, source_target_pairs={{0,2},{1,3},{2,0},{3,1},{4,6},{5,7},{6,4},{7,5},{8,10},{9,11},{10,... | collective-permute-start | bytes 1572872 | tf_op jit(solution)/shard_map/ppermute | solution.py:190
  111.2 2.5 %collective-permute-start.9 = (f32[128,256]{1,0:T(8,128)S(1)}, f32[128,256]{1,0:T(8,128)S(1)}, u32[]{:S(2)}, u32[]{:S(2)}) collective-permute-start(f32[128,256]{1,0:T(8,128)S(1)} %get-tuple-element.26), channel_id=1, source_target_pairs={{0,3},{1,0},{2,1},{3,2},{4,7},{5,4},{6,5},{7,6},{8,11},{9,8},{10,9... | collective-permute-start | bytes 393224 | tf_op jit(solution)/shard_map/ppermute | solution.py:190
  113.7 10.0 %collective-permute-done.13 = f32[4,128,256]{2,1,0:T(8,128)S(1)} collective-permute-done((f32[4,128,256]{2,1,0:T(8,128)S(1)}, f32[4,128,256]{2,1,0:T(8,128)S(1)}, u32[]{:S(2)}, u32[]{:S(2)}) %collective-permute-start.13) | collective-permute-done | bytes 524320 | tf_op jit(solution)/shard_map/ppermute | solution.py:190
  125.1 2.2 %collective-permute-start.15 = (f32[128,256]{1,0:T(8,128)S(1)}, f32[128,256]{1,0:T(8,128)S(1)}, u32[]{:S(2)}, u32[]{:S(2)}) collective-permute-start(f32[128,256]{1,0:T(8,128)S(1)} %get-tuple-element.29), channel_id=1, source_target_pairs={{0,12},{1,13},{2,14},{3,15},{4,0},{5,1},{6,2},{7,3},{8,4},{9,5},{1... | collective-permute-start | bytes 393224 | tf_op jit(solution)/shard_map/ppermute | solution.py:190
  127.3 4.3 %collective-permute-done.14 = f32[128,256]{1,0:T(8,128)S(1)} collective-permute-done((f32[128,256]{1,0:T(8,128)S(1)}, f32[128,256]{1,0:T(8,128)S(1)}, u32[]{:S(2)}, u32[]{:S(2)}) %collective-permute-start.14) | collective-permute-done | bytes 131104 | tf_op jit(solution)/shard_map/ppermute | solution.py:190
  (48 shorter events, 8.7 us)
Async XLA Ops:
  12.3 11.2 %copy-start.4 = (s32[128,512]{1,0:T(8,128)S(1)}, s32[128,512]{1,0:T(8,128)}, u32[]{:S(2)}) copy-start(s32[128,512]{1,0:T(8,128)} %slot_ref.1) | copy-start | bytes 786436
  12.3 35.6 %copy-start.3 = (f32[2,128,256]{2,1,0:T(8,128)S(1)}, f32[2,128,256]{2,1,0:T(8,128)}, u32[]{:S(2)}) copy-start(f32[2,128,256]{2,1,0:T(8,128)} %parent_ref.1) | copy-start | bytes 786436
  12.3 35.6 %all-to-all-start = ((f32[128,24,128]{2,1,0:T(8,128)}), f32[128,24,128]{2,1,0:T(8,128)S(1)}, u32[]{:S(2)}, u32[]{:S(2)}) async-start(f32[128,24,128]{2,1,0:T(8,128)} %bitcast.9), calls=%async_computation | async-start | bytes 3145728 | tf_op jit(solution)/shard_map/all_to_all | solution.py:240
  48.6 10.8 %collective-permute-start.3 = (f32[128,512]{1,0:T(8,128)S(1)}, f32[128,512]{1,0:T(8,128)S(1)}, u32[]{:S(2)}, u32[]{:S(2)}) collective-permute-start(f32[128,512]{1,0:T(8,128)S(1)} %extend.1.own_ref), channel_id=1, source_target_pairs={{0,64},{16,80},{32,96},{48,112},{64,0},{80,16},{96,32},{112,48},{1... | collective-permute-start | bytes 786440 | tf_op jit(solution)/shard_map/ppermute | solution.py:190
  49.5 12.3 %collective-permute-start.2 = (f32[128,512]{1,0:T(8,128)S(1)}, f32[128,512]{1,0:T(8,128)S(1)}, u32[]{:S(2)}, u32[]{:S(2)}) collective-permute-start(f32[128,512]{1,0:T(8,128)S(1)} %extend.1.own_ref), channel_id=1, source_target_pairs={{0,96},{16,112},{32,0},{48,16},{64,32},{80,48},{96,64},{112,80},{1... | collective-permute-start | bytes 786440 | tf_op jit(solution)/shard_map/ppermute | solution.py:190
  52.1 10.8 %collective-permute-start.1 = (f32[128,512]{1,0:T(8,128)S(1)}, f32[128,512]{1,0:T(8,128)S(1)}, u32[]{:S(2)}, u32[]{:S(2)}) collective-permute-start(f32[128,512]{1,0:T(8,128)S(1)} %extend.1.own_ref), channel_id=1, source_target_pairs={{0,32},{16,48},{32,64},{48,80},{64,96},{80,112},{96,0},{112,16},{1... | collective-permute-start | bytes 786440 | tf_op jit(solution)/shard_map/ppermute | solution.py:190
  62.9 2.7 %collective-permute-start.4 = (f32[3,128,512]{2,1,0:T(8,128)S(1)}, f32[3,128,512]{2,1,0:T(8,128)S(1)}, u32[]{:S(2)}, u32[]{:S(2)}) collective-permute-start(f32[3,128,512]{2,1,0:T(8,128)S(1)} %pad_maximum_fusion), channel_id=1, source_target_pairs={{0,16},{16,0},{32,48},{48,32},{64,80},{80,64},{96,112},{112,96},{1... | collective-permute-start | bytes 2359304 | tf_op jit(solution)/shard_map/ppermute | solution.py:190
  63.0 2.6 %collective-permute-start = (f32[128,512]{1,0:T(8,128)S(1)}, f32[128,512]{1,0:T(8,128)S(1)}, u32[]{:S(2)}, u32[]{:S(2)}) collective-permute-start(f32[128,512]{1,0:T(8,128)S(1)} %extend.1.own_ref), channel_id=1, source_target_pairs={{0,16},{16,0},{32,48},{48,32},{64,80},{80,64},{96,112},{112,96},{1... | collective-permute-start | bytes 786440 | tf_op jit(solution)/shard_map/ppermute | solution.py:190
  80.8 26.5 %collective-permute-start.5 = (f32[4,128,256]{2,1,0:T(8,128)S(1)}, f32[4,128,256]{2,1,0:T(8,128)S(1)}, u32[]{:S(2)}, u32[]{:S(2)}) collective-permute-start(f32[4,128,256]{2,1,0:T(8,128)S(1)} %get-tuple-element.14), channel_id=1, source_target_pairs={{0,4},{1,5},{2,6},{3,7},{4,8},{5,9},{6,10},{7,11},{8,12},{9,13},{1... | collective-permute-start | bytes 1572872 | tf_op jit(solution)/shard_map/ppermute | solution.py:190
  81.8 27.6 %collective-permute-start.6 = (f32[4,128,256]{2,1,0:T(8,128)S(1)}, f32[4,128,256]{2,1,0:T(8,128)S(1)}, u32[]{:S(2)}, u32[]{:S(2)}) collective-permute-start(f32[4,128,256]{2,1,0:T(8,128)S(1)} %get-tuple-element.15), channel_id=1, source_target_pairs={{0,12},{1,13},{2,14},{3,15},{4,0},{5,1},{6,2},{7,3},{8,4},{9,5},{1... | collective-permute-start | bytes 1572872 | tf_op jit(solution)/shard_map/ppermute | solution.py:190
  84.1 25.3 %collective-permute-start.7 = (f32[4,128,256]{2,1,0:T(8,128)S(1)}, f32[4,128,256]{2,1,0:T(8,128)S(1)}, u32[]{:S(2)}, u32[]{:S(2)}) collective-permute-start(f32[4,128,256]{2,1,0:T(8,128)S(1)} %get-tuple-element.16), channel_id=1, source_target_pairs={{0,8},{1,9},{2,10},{3,11},{4,12},{5,13},{6,14},{7,15},{8,0},{9,1},... | collective-permute-start | bytes 1572872 | tf_op jit(solution)/shard_map/ppermute | solution.py:190
  85.2 26.0 %collective-permute-start.11 = (f32[4,128,256]{2,1,0:T(8,128)S(1)}, f32[4,128,256]{2,1,0:T(8,128)S(1)}, u32[]{:S(2)}, u32[]{:S(2)}) collective-permute-start(f32[4,128,256]{2,1,0:T(8,128)S(1)} %get-tuple-element.18), channel_id=1, source_target_pairs={{0,1},{1,2},{2,3},{3,0},{4,5},{5,6},{6,7},{7,4},{8,9},{9,10},{10,1... | collective-permute-start | bytes 1572872 | tf_op jit(solution)/shard_map/ppermute | solution.py:190
  86.0 27.7 %collective-permute-start.12 = (f32[4,128,256]{2,1,0:T(8,128)S(1)}, f32[4,128,256]{2,1,0:T(8,128)S(1)}, u32[]{:S(2)}, u32[]{:S(2)}) collective-permute-start(f32[4,128,256]{2,1,0:T(8,128)S(1)} %get-tuple-element.19), channel_id=1, source_target_pairs={{0,3},{1,0},{2,1},{3,2},{4,7},{5,4},{6,5},{7,6},{8,11},{9,8},{10,9... | collective-permute-start | bytes 1572872 | tf_op jit(solution)/shard_map/ppermute | solution.py:190
  107.3 16.5 %collective-permute-start.13 = (f32[4,128,256]{2,1,0:T(8,128)S(1)}, f32[4,128,256]{2,1,0:T(8,128)S(1)}, u32[]{:S(2)}, u32[]{:S(2)}) collective-permute-start(f32[4,128,256]{2,1,0:T(8,128)S(1)} %get-tuple-element.20), channel_id=1, source_target_pairs={{0,2},{1,3},{2,0},{3,1},{4,6},{5,7},{6,4},{7,5},{8,10},{9,11},{10,... | collective-permute-start | bytes 1572872 | tf_op jit(solution)/shard_map/ppermute | solution.py:190
  109.7 15.4 %collective-permute-start.8 = (f32[128,256]{1,0:T(8,128)S(1)}, f32[128,256]{1,0:T(8,128)S(1)}, u32[]{:S(2)}, u32[]{:S(2)}) collective-permute-start(f32[128,256]{1,0:T(8,128)S(1)} %get-tuple-element.24), channel_id=1, source_target_pairs={{0,1},{1,2},{2,3},{3,0},{4,5},{5,6},{6,7},{7,4},{8,9},{9,10},{10,1... | collective-permute-start | bytes 393224 | tf_op jit(solution)/shard_map/ppermute | solution.py:190
  110.5 16.8 %collective-permute-start.10 = (f32[128,256]{1,0:T(8,128)S(1)}, f32[128,256]{1,0:T(8,128)S(1)}, u32[]{:S(2)}, u32[]{:S(2)}) collective-permute-start(f32[128,256]{1,0:T(8,128)S(1)} %get-tuple-element.25), channel_id=1, source_target_pairs={{0,2},{1,3},{2,0},{3,1},{4,6},{5,7},{6,4},{7,5},{8,10},{9,11},{10,... | collective-permute-start | bytes 393224 | tf_op jit(solution)/shard_map/ppermute | solution.py:190
  111.2 16.1 %collective-permute-start.9 = (f32[128,256]{1,0:T(8,128)S(1)}, f32[128,256]{1,0:T(8,128)S(1)}, u32[]{:S(2)}, u32[]{:S(2)}) collective-permute-start(f32[128,256]{1,0:T(8,128)S(1)} %get-tuple-element.26), channel_id=1, source_target_pairs={{0,3},{1,0},{2,1},{3,2},{4,7},{5,4},{6,5},{7,6},{8,11},{9,8},{10,9... | collective-permute-start | bytes 393224 | tf_op jit(solution)/shard_map/ppermute | solution.py:190
  123.8 8.9 %copy-start.6 = (f32[3,128]{1,0:T(4,128)S(1)}, f32[3,128]{1,0:T(4,128)}, u32[]{:S(2)}) copy-start(f32[3,128]{1,0:T(4,128)} %param.20) | copy-start | bytes 4612
  123.8 8.9 %copy-start.7 = (f32[128]{0:T(128)S(1)}, f32[128]{0:T(128)}, u32[]{:S(2)}) copy-start(f32[128]{0:T(128)} %param.22) | copy-start | bytes 1540
  123.8 8.9 %copy-start.8 = (f32[128]{0:T(128)S(1)}, f32[128]{0:T(128)}, u32[]{:S(2)}) copy-start(f32[128]{0:T(128)} %param.23) | copy-start | bytes 1540
  123.8 9.0 %copy-start.9 = (f32[128]{0:T(128)S(1)}, f32[128]{0:T(128)}, u32[]{:S(2)}) copy-start(f32[128]{0:T(128)} %param.21) | copy-start | bytes 1540
  124.0 7.7 %collective-permute-start.14 = (f32[128,256]{1,0:T(8,128)S(1)}, f32[128,256]{1,0:T(8,128)S(1)}, u32[]{:S(2)}, u32[]{:S(2)}) collective-permute-start(f32[128,256]{1,0:T(8,128)S(1)} %get-tuple-element.27), channel_id=1, source_target_pairs={{0,4},{1,5},{2,6},{3,7},{4,8},{5,9},{6,10},{7,11},{8,12},{9,13},{1... | collective-permute-start | bytes 393224 | tf_op jit(solution)/shard_map/ppermute | solution.py:190
  124.1 7.6 %collective-permute-start.16 = (f32[128,256]{1,0:T(8,128)S(1)}, f32[128,256]{1,0:T(8,128)S(1)}, u32[]{:S(2)}, u32[]{:S(2)}) collective-permute-start(f32[128,256]{1,0:T(8,128)S(1)} %get-tuple-element.28), channel_id=1, source_target_pairs={{0,8},{1,9},{2,10},{3,11},{4,12},{5,13},{6,14},{7,15},{8,0},{9,1},... | collective-permute-start | bytes 393224 | tf_op jit(solution)/shard_map/ppermute | solution.py:190
  125.1 7.4 %collective-permute-start.15 = (f32[128,256]{1,0:T(8,128)S(1)}, f32[128,256]{1,0:T(8,128)S(1)}, u32[]{:S(2)}, u32[]{:S(2)}) collective-permute-start(f32[128,256]{1,0:T(8,128)S(1)} %get-tuple-element.29), channel_id=1, source_target_pairs={{0,12},{1,13},{2,14},{3,15},{4,0},{5,1},{6,2},{7,3},{8,4},{9,5},{1... | collective-permute-start | bytes 393224 | tf_op jit(solution)/shard_map/ppermute | solution.py:190
  (4 other events, 5.7 us)
